TPU v7x, 32 devices: a whole 2x2x4 slice. The times are simulated.
32 devices in a mesh: scene: 8 (over y, x, core), batch: 4 (over z).
Axes of the slice: x: 2, y: 2, z: 4, core: 2. Of those that a mesh axis runs over, the one named last changes fastest.
Arguments:
- tokens: float32 [4, 3072, 384], P('batch', 'scene'), may hold values from -6 to 6
- nbr_offset: int32 [27, 4, 3072], P(None, 'batch', 'scene'), may hold values from -64 to 65, as said below
- cotangent: float32 [4, 3072, 384], P('batch', 'scene'), may hold values from -6 to 6
- conv_weight: float32 [27, 384], replicated, may hold values from -1.25 to 1.25
- w_qkv: float32 [384, 1152], replicated, may hold values from -0.3125 to 0.3125
- w_out: float32 [384, 384], replicated, may hold values from -0.3125 to 0.3125
- score_bias: float32 [24, 32, 32], replicated, may hold values from -6 to 400
- w_up: float32 [384, 1536], replicated, may hold values from -0.3125 to 0.3125
- w_down: float32 [1536, 384], replicated, may hold values from -0.15625 to 0.15625
Outputs:
- block_out: float32 [4, 3072, 384], P('batch', 'scene')
- grad_mid: float32 [4, 3072, 384], P('batch', 'scene')
- grad_up: float32 [384, 1536], P('scene', 'batch')
- grad_down: float32 [1536, 384], P('scene', 'batch')
Inputs may be any that keep to these rules, and one draw needn't show every extreme that they name: `nbr_offset`: the middle tap is 0 for every token; the value 64 + 1 marks a missing neighbour.
All inputs are finite; a program needn't handle non-finite values.
Results may differ from a plain program's by a relative error of at most 0.000075.
Values sent between devices are 32-bit elements; how exact they have to be, the bound alone decides.
A program may use at most 128 MiB of HBM per device.

v0:
```python
import functools

import jax
import jax.numpy as jnp
import numpy as np
from jax import lax
from jax.experimental import pallas as pl
from jax.experimental.pallas import tpu as pltpu
from jax.sharding import PartitionSpec as P

GROUP = 32
HALO = 64
TILE = 128
F32 = jnp.float32
BF16 = jnp.bfloat16
VMEM_LIMIT = 56 * 1024 * 1024


def split(x):
    hi = x.astype(BF16)
    return hi, (x - hi.astype(F32)).astype(BF16)


def left3(x, axis=1):
    hi, lo = split(x)
    return jnp.concatenate([hi, hi, lo], axis=axis)


def right3(x, axis=0):
    hi, lo = split(x)
    return jnp.concatenate([hi, lo, hi], axis=axis)


def dot(a, b):
    return lax.dot_general(a, b, (((1,), (0,)), ((), ())), preferred_element_type=F32)


def dot_t(a, b):
    return lax.dot_general(a, b, (((1,), (1,)), ((), ())), preferred_element_type=F32)


def norm_of(values):
    average = jnp.mean(values, axis=-1, keepdims=True)
    centered = values - average
    variance = jnp.mean(centered * centered, axis=-1, keepdims=True)
    scale = lax.rsqrt(variance + 1e-05)
    return centered * scale, scale


def conv_kernel(local_ref, low_ref, high_ref, offset_ref, weight_ref, first_ref, normed_ref, ext, off_t):
    tok, width = local_ref.shape
    taps = weight_ref.shape[0]
    for start, ref in ((0, low_ref), (HALO, local_ref), (HALO + tok, high_ref)):
        hi, lo = split(ref[...])
        ext[pl.ds(start, ref.shape[0]), :width] = hi
        ext[pl.ds(start, ref.shape[0]), width:] = lo
    for b in range(tok // TILE):
        piece = offset_ref[:, b * TILE : (b + 1) * TILE]
        piece = jnp.where(piece > HALO, 4 * TILE, piece).astype(F32)
        piece = jnp.concatenate([piece, jnp.zeros((TILE - taps, TILE), F32)], axis=0)
        off_t[b * TILE : (b + 1) * TILE, :] = piece.T
    span = TILE + 2 * HALO
    base = (
        lax.broadcasted_iota(jnp.int32, (TILE, span), 1)
        - lax.broadcasted_iota(jnp.int32, (TILE, span), 0)
        - HALO
    ).astype(F32)

    @pl.loop(0, tok // TILE)
    def _(b):
        row = pl.multiple_of(b * TILE, TILE)
        window = ext[pl.ds(row, span), :]
        offsets = off_t[pl.ds(row, TILE), :]
        total = local_ref[pl.ds(row, TILE), :]
        for a in range(taps):
            pick = jnp.where(base == offsets[:, a : a + 1], 1.0, 0.0).astype(BF16)
            found = dot(pick, window)
            total += (found[:, :width] + found[:, width:]) * weight_ref[a : a + 1, :]
        first_ref[pl.ds(row, TILE), :] = total
        normed_ref[pl.ds(row, TILE), :] = norm_of(total)[0]


def attend_kernel(head_dim, x_ref, perm_ref, back_ref, wqkv_ref, wout_ref, bias_ref, out_ref, qkv, att):
    tok, width = x_ref.shape
    hi, lo = split(x_ref[...])
    hi = dot(perm_ref[...], hi).astype(BF16)
    lo = dot(perm_ref[...], lo).astype(BF16)
    rows3 = jnp.concatenate([hi, hi, lo], axis=1)
    for part in range(3):
        qkv[:, part * width : (part + 1) * width] = dot(
            rows3, right3(wqkv_ref[:, part * width : (part + 1) * width])
        )
    per_lane = TILE // head_dim
    shape = (TILE, TILE)
    same = (lax.broadcasted_iota(jnp.int32, shape, 0) ^ lax.broadcasted_iota(jnp.int32, shape, 1)) < GROUP
    away = jnp.where(same, 0.0, -1e30)
    lane = lax.broadcasted_iota(jnp.int32, shape, 1)

    @pl.loop(0, tok // TILE)
    def _(b):
        row = pl.ds(pl.multiple_of(b * TILE, TILE), TILE)
        for part in range(width // TILE):
            at = part * TILE
            q = qkv[row, at : at + TILE] * (head_dim**-0.5)
            k = qkv[row, width + at : width + at + TILE]
            v = qkv[row, 2 * width + at : 2 * width + at + TILE]
            keys, values = [], []
            for h in range(per_lane):
                mine = (lane >= h * head_dim) & (lane < (h + 1) * head_dim)
                keys.append(right3(jnp.where(mine, k, 0.0), axis=1))
                values.append(jnp.concatenate(split(jnp.where(mine, v, 0.0)), axis=1))
            scores = dot_t(left3(q), jnp.concatenate(keys, axis=0))
            his, los = [], []
            for h in range(per_lane):
                bias = jnp.concatenate([bias_ref[part * per_lane + h]] * (TILE // GROUP), axis=0)
                s = scores[:, h * TILE : (h + 1) * TILE] + bias + away
                e = jnp.exp(s - jnp.max(s, axis=-1, keepdims=True))
                p = e / jnp.sum(e, axis=-1, keepdims=True)
                p_hi, p_lo = split(p)
                his.append(p_hi)
                los.append(p_lo)
            values = jnp.concatenate(values, axis=0)
            both = dot(jnp.concatenate(his, axis=1), values)
            rest = dot(jnp.concatenate(los, axis=1), values[:, :TILE])
            att[row, at : at + TILE] = both[:, :TILE] + both[:, TILE:] + rest

    hi, lo = split(att[...])
    hi = dot(back_ref[...], hi).astype(BF16)
    lo = dot(back_ref[...], lo).astype(BF16)
    out_ref[...] = dot(jnp.concatenate([hi, hi, lo], axis=1), right3(wout_ref[...]))


def mlp_kernel(
    grad_scale, first_ref, mixed_ref, cot_ref, up_ref, down_ref,
    out_ref, mid_ref, gup_ref, gdown_ref,
    n_left, c_left, nt_left, ct_left, grad_normed,
):
    tok, width = first_ref.shape
    hidden_width = up_ref.shape[1]
    chunk = 2 * TILE
    middle = first_ref[...] + mixed_ref[...]
    normed, scale = norm_of(middle)
    cot = cot_ref[...]
    n_left[...] = left3(normed)
    c_left[...] = left3(cot)
    nt_left[...] = left3(normed.T * grad_scale)
    ct_left[...] = left3(cot.T * grad_scale)
    out_ref[...] = middle
    grad_normed[...] = jnp.zeros_like(grad_normed)

    @pl.loop(0, hidden_width // chunk)
    def _(c):
        at = pl.ds(pl.multiple_of(c * chunk, chunk), chunk)
        up_hi, up_lo = split(up_ref[:, at])
        down_hi, down_lo = split(down_ref[at, :])
        hidden = dot(n_left[...], jnp.concatenate([up_hi, up_lo, up_hi], axis=0))
        grad_act = dot_t(c_left[...], jnp.concatenate([down_hi, down_lo, down_hi], axis=1))
        cdf = 0.5 * (1.0 + lax.erf(hidden * (0.5**0.5)))
        act = hidden * cdf
        density = jnp.exp(-0.5 * hidden * hidden) * ((2.0 * np.pi) ** -0.5)
        grad_hidden = grad_act * (cdf + hidden * density)
        act_hi, act_lo = split(act)
        gh_hi, gh_lo = split(grad_hidden)
        gup_ref[:, at] = dot(nt_left[...], jnp.concatenate([gh_hi, gh_lo, gh_hi], axis=0))
        gdown_ref[at, :] = dot(ct_left[...], jnp.concatenate([act_hi, act_lo, act_hi], axis=0)).T
        out_ref[...] += dot(
            jnp.concatenate([act_hi, act_hi, act_lo], axis=1),
            jnp.concatenate([down_hi, down_lo, down_hi], axis=0),
        )
        grad_normed[...] += dot_t(
            jnp.concatenate([gh_hi, gh_hi, gh_lo], axis=1),
            jnp.concatenate([up_hi, up_lo, up_hi], axis=1),
        )

    g = grad_normed[...]
    along = jnp.mean(g * normed, axis=-1, keepdims=True)
    mid_ref[...] = cot + scale * (g - jnp.mean(g, axis=-1, keepdims=True) - normed * along)


def shape_of(*dims):
    return jax.ShapeDtypeStruct(dims, F32)


def call(kernel, outs, scratch, flops):
    return pl.pallas_call(
        kernel,
        out_shape=outs,
        scratch_shapes=scratch,
        compiler_params=pltpu.CompilerParams(vmem_limit_bytes=VMEM_LIMIT),
        cost_estimate=pl.CostEstimate(flops=flops, bytes_accessed=4000000, transcendentals=0),
    )


def orders(tok, scene_count):
    per, count = GROUP // scene_count, tok // GROUP
    row = np.arange(tok)
    group, slot = row // GROUP, row % GROUP
    source = ((slot % per) * scene_count + slot // per) * count + group
    perm = np.zeros((tok, tok), np.float32)
    perm[row, source] = 1.0
    return perm


def on_device(tokens, nbr_offset, cotangent, conv_weight, w_qkv, w_out, score_bias, w_up, w_down):
    local = tokens[0]
    tok, width = local.shape
    hidden_width = w_up.shape[1]
    heads = score_bias.shape[0]
    scene_count = lax.axis_size("scene")
    batch_count = lax.axis_size("batch")
    forward = [(i, i + 1) for i in range(scene_count - 1)]
    backward = [(target, source) for source, target in forward]
    low = lax.ppermute(local[tok - HALO :], "scene", forward)
    high = lax.ppermute(local[:HALO], "scene", backward)
    first, normed = call(
        conv_kernel,
        (shape_of(tok, width), shape_of(tok, width)),
        [pltpu.VMEM((tok + 2 * HALO, 2 * width), BF16), pltpu.VMEM((tok, TILE), F32)],
        8 * 10**9,
    )(local, low, high, nbr_offset[:, 0, :], conv_weight)
    per, count = GROUP // scene_count, tok // GROUP
    blocks = normed.reshape(per, scene_count, count, width)
    arrived = lax.all_to_all(blocks, "scene", split_axis=1, concat_axis=1, tiled=True)
    perm = orders(tok, scene_count)
    bias = jnp.tile(score_bias, (1, 1, TILE // GROUP))
    mixed = call(
        functools.partial(attend_kernel, width // heads),
        shape_of(tok, width),
        [pltpu.VMEM((tok, 3 * width), F32), pltpu.VMEM((tok, width), F32)],
        10**10,
    )(
        arrived.reshape(tok, width),
        jnp.asarray(perm, BF16),
        jnp.asarray(perm.T, BF16),
        w_qkv,
        w_out,
        bias,
    )
    returned = lax.all_to_all(
        mixed.reshape(per, scene_count, count, width), "scene", split_axis=1, concat_axis=1, tiled=True
    ).reshape(tok, width)
    grad_scale = float(tok * scene_count * batch_count) ** -0.5
    block_out, grad_mid, grad_up, grad_down = call(
        functools.partial(mlp_kernel, grad_scale),
        (
            shape_of(tok, width),
            shape_of(tok, width),
            shape_of(width, hidden_width),
            shape_of(hidden_width, width),
        ),
        [pltpu.VMEM((tok, 3 * width), BF16)] * 2
        + [pltpu.VMEM((width, 3 * tok), BF16)] * 2
        + [pltpu.VMEM((tok, width), F32)],
        10**10,
    )(first, returned, cotangent[0], w_up, w_down)
    grads = []
    for grad in (grad_up, grad_down):
        part = lax.psum_scatter(grad, "scene", scatter_dimension=0, tiled=True)
        grads.append(lax.psum_scatter(part, "batch", scatter_dimension=1, tiled=True))
    return (block_out[None], grad_mid[None], *grads)


def solution(mesh):
    tokens = P("batch", "scene", None)
    return jax.shard_map(
        on_device,
        mesh=mesh,
        in_specs=(tokens, P(None, "batch", "scene"), tokens) + (P(),) * 6,
        out_specs=(tokens, tokens, P("scene", "batch"), P("scene", "batch")),
        check_vma=False,
    )
```

profile of v0, /device:TPU:0, one launch (start us, length us, event | category | flops | bytes accessed | tf_op | source)
XLA Modules:
  0.0 228.6 jit_solution(9626661922471600453)
XLA Ops:
  7.2 1.0 slice_bitcast_fusion
  8.1 1.3 collective-permute-start.1
  9.4 3.0 %collective-permute-start = (f32[64,384]{1,0:T(8,128)S(1)}, f32[64,384]{1,0:T(8,128)S(1)}, u32[]{:S(2)}, u32[]{:S(2)}) collective-permute-start(f32[64,384]{1,0:T(8,128)S(1)} %get-tuple-element.17), channel_id=1, source_target_pairs={{0,4},{4,8},{8,12},{12,16},{16,20},{20,24},{24,28},{1,5},{5,9},{9,... | collective-permute-start | bytes 294920 | tf_op jit(solution)/shard_map/ppermute | solution.py:213
  12.5 1.4 copy.23
  13.9 0.6 copy-done.1
  14.6 7.7 %shard_map.138 = (f32[384,384]{1,0:T(8,128)}, f32[384,384]{1,0:T(8,128)}) custom-call(f32[384,384]{1,0:T(8,128)} %bitcast.15, f32[64,384]{1,0:T(8,128)} %copy-done.2, f32[64,384]{1,0:T(8,128)} %copy-done.1, s32[27,384]{1,0:T(8,128)} %bitcast.16, f32[27,384]{1,0:T(8,128)} %weight_ref.1), custom_call_target="tpu_custom_call" | custom-call | flops 8000000000 | bytes 4000000 | tf_op jit(solution)/shard_map/pallas_call | solution.py:215
  22.3 1.2 reshape.26
  23.5 1.2 copy.15
  24.7 8.1 %all-to-all-start = ((f32[4,8,12,384]{3,0,2,1:T(4,128)}), f32[4,8,12,384]{3,0,2,1:T(4,128)S(1)}, u32[]{:S(2)}, u32[]{:S(2)}) async-start(f32[4,8,12,384]{3,0,2,1:T(4,128)} %copy.15), calls=%async_computation | async-start | bytes 1179648 | tf_op jit(solution)/shard_map/all_to_all | solution.py:223
  33.1 1.4 tile.10.bias_ref
  34.5 8.7 %all-to-all-done = f32[4,8,12,384]{3,0,2,1:T(4,128)S(1)} async-done(((f32[4,8,12,384]{3,0,2,1:T(4,128)}), f32[4,8,12,384]{3,0,2,1:T(4,128)S(1)}, u32[]{:S(2)}, u32[]{:S(2)}) %all-to-all-start) | async-done | bytes 589856 | tf_op jit(solution)/shard_map/all_to_all | solution.py:223
  43.3 0.9 reshape.27.x_ref
  44.2 12.4 %shard_map.139 = f32[384,384]{1,0:T(8,128)} custom-call(f32[384,384]{1,0:T(8,128)} %reshape.27.x_ref, bf16[384,384]{1,0:T(8,128)(2,1)} %constant.4.clone.perm_ref, bf16[384,384]{1,0:T(8,128)(2,1)} %constant.5.clone.back_ref, f32[384,1152]{1,0:T(8,128)} %wqkv_ref.1, f32[384,384]{1,0:T(8,128)} %wout_ref.1, f32[24,32,128]{2,1,0:T(8,128)} %tile.10.bias_ref), custom_call_target="tpu_custom_call" | custom-call | flops 10000000000 | bytes 4000000 | tf_op jit(solution)/shard_map/pallas_call | solution.py:226
  56.6 1.1 reshape.28
  58.1 12.8 %all_to_all.10 = f32[4,8,12,384]{3,0,2,1:T(4,128)S(1)} all-to-all(f32[4,8,12,384]{3,0,2,1:T(4,128)S(1)} %copy.17), channel_id=1, replica_groups=mesh['scene'=8,'batch'=4] {'scene'}, dimensions={1} | all-to-all | bytes 1179648 | tf_op jit(solution)/shard_map/all_to_all | solution.py:239
  71.0 0.9 reshape.29.mixed_ref
  71.9 17.9 %shard_map.140 = (f32[384,384]{1,0:T(8,128)}, f32[384,384]{1,0:T(8,128)}, f32[384,1536]{1,0:T(8,128)}, f32[1536,384]{1,0:T(8,128)}) custom-call(f32[384,384]{1,0:T(8,128)} %get-tuple-element.10.first_ref, f32[384,384]{1,0:T(8,128)} %reshape.29.mixed_ref, f32[384,384]{1,0:T(8,128)} %bitcast.17, f32[384,1536]{1,0:T(8,128)} %up_ref.1, f32[1536,384]{1,0:T(8,128)} %down_ref.1), custom_call_target="tpu_custom_call" | custom-call | flops 10000000000 | bytes 4000000 | tf_op jit(solution)/shard_map/pallas_call | solution.py:243
  89.9 0.7 reduce-scatter.7.cloned.1.call-update
  90.7 41.2 %reduce-scatter.11.cloned.1.call-done = f32[192,384]{1,0:T(8,128)} async-done(((f32[1536,384]{1,0:T(8,128)}), f32[192,384]{1,0:T(8,128)}) %reduce-scatter.11.cloned.1.call-update) | async-done | bytes 294928 | tf_op jit(solution)/shard_map/reduce_scatter | solution.py:258
  131.9 1.9 copy.19
  133.9 44.3 %reduce-scatter.7.cloned.1.call-done = f32[48,1536]{1,0:T(8,128)} async-done(((f32[384,1536]{1,0:T(8,128)}), f32[48,1536]{1,0:T(8,128)}) %reduce-scatter.7.cloned.1.call-update) | async-done | bytes 294928 | tf_op jit(solution)/shard_map/reduce_scatter | solution.py:258
  178.2 22.9 %reduce-scatter.13.cloned.1.call-done = f32[96,192]{1,0:T(8,128)} async-done(((f32[384,192]{1,0:T(8,128)}), f32[96,192]{1,0:T(8,128)}) %reduce-scatter.13.cloned.1.call-update) | async-done | bytes 73744
  201.0 1.6 copy.20
  202.7 19.4 %reduce-scatter.9.cloned.1.call-done = f32[48,384]{1,0:T(8,128)} async-done(((f32[48,1536]{1,0:T(8,128)}), f32[48,384]{1,0:T(8,128)}) %reduce-scatter.9.cloned.1.call-update) | async-done | bytes 73744 | tf_op jit(solution)/shard_map/reduce_scatter | solution.py:259
  (18 shorter events, 1.1 us)
Async XLA Ops:
  8.1 5.8 %collective-permute-start.1 = (f32[64,384]{1,0:T(8,128)S(1)}, f32[64,384]{1,0:T(8,128)S(1)}, u32[]{:S(2)}, u32[]{:S(2)}) collective-permute-start(f32[64,384]{1,0:T(8,128)S(1)} %get-tuple-element.16), channel_id=1, source_target_pairs={{4,0},{8,4},{12,8},{16,12},{20,16},{24,20},{28,24},{5,1},{9,5},{13... | collective-permute-start | bytes 294920 | tf_op jit(solution)/shard_map/ppermute | solution.py:214
  9.4 4.5 %collective-permute-start = (f32[64,384]{1,0:T(8,128)S(1)}, f32[64,384]{1,0:T(8,128)S(1)}, u32[]{:S(2)}, u32[]{:S(2)}) collective-permute-start(f32[64,384]{1,0:T(8,128)S(1)} %get-tuple-element.17), channel_id=1, source_target_pairs={{0,4},{4,8},{8,12},{12,16},{16,20},{20,24},{24,28},{1,5},{5,9},{9,... | collective-permute-start | bytes 294920 | tf_op jit(solution)/shard_map/ppermute | solution.py:213
  13.9 0.6 copy-start.1
  13.9 0.7 copy-start.2
  22.3 10.5 %copy-start = (f32[24,32,32]{2,1,0:T(8,128)S(1)}, f32[24,32,32]{2,1,0:T(8,128)}, u32[]{:S(2)}) copy-start(f32[24,32,32]{2,1,0:T(8,128)} %param.17) | copy-start | bytes 294916
  24.7 18.5 %all-to-all-start = ((f32[4,8,12,384]{3,0,2,1:T(4,128)}), f32[4,8,12,384]{3,0,2,1:T(4,128)S(1)}, u32[]{:S(2)}, u32[]{:S(2)}) async-start(f32[4,8,12,384]{3,0,2,1:T(4,128)} %copy.15), calls=%async_computation | async-start | bytes 1179648 | tf_op jit(solution)/shard_map/all_to_all | solution.py:223
  32.8 99.2 %reduce-scatter.11.cloned.1.call-start = ((), (), s32[]{:S(2)}) async-start(), calls=%async_computation.8 | async-start | bytes 2654208 | tf_op jit(solution)/shard_map/reduce_scatter | solution.py:258
  89.9 88.2 %reduce-scatter.7.cloned.1.call-start = ((), (), s32[]{:S(2)}) async-start(), calls=%async_computation.6 | async-start | bytes 2654208 | tf_op jit(solution)/shard_map/reduce_scatter | solution.py:258
  90.6 110.4 %reduce-scatter.13.cloned.1.call-start = ((), (), s32[]{:S(2)}) async-start(), calls=%async_computation.9 | async-start | bytes 491520
  133.8 88.2 %reduce-scatter.9.cloned.1.call-start = ((), (), s32[]{:S(2)}) async-start(), calls=%async_computation.7 | async-start | bytes 368640 | tf_op jit(solution)/shard_map/reduce_scatter | solution.py:259
Sparse Core Ops, SparseCore 0:
  90.0 41.8 reduce-scatter.10
  135.6 42.4 reduce-scatter.6
  180.4 20.5 reduce-scatter.12
  203.8 18.1 reduce-scatter.8
where the time goes:
time: 229 us
  waiting for transfers between devices  137 us (60%)
  Pallas kernels  38.1 us (17%)
  local copies, waits for them, and re-layouts  14 us (6%)
  between operations  13.8 us (6%)
  blocking collectives  12.8 us (6%)
  starting transfers between devices  12.6 us (6%)
    reduce_scatter x2, waiting for transfers between devices, on_device(): part = lax.psum_scatter(grad, 'scene', scatter_dimension=0, tiled=True)  85.5 us
    unnamed x5, waiting for transfers between devices  23.6 us
    reduce_scatter x1, waiting for transfers between devices, on_device(): lax.psum_scatter(part, 'batch', scatter_dimension=1, tiled=True)  19.4 us
    pallas_call x1, Pallas kernels, on_device(): call(functools.partial(mlp_kernel, grad_scale), (shape_of(tok, width), sh...  17.9 us
    all_to_all x1, blocking collectives, on_device(): lax.all_to_all(mixed.reshape(per, scene_count, count, width), 'scene', sp...  12.8 us
    pallas_call x1, Pallas kernels, on_device(): call(functools.partial(attend_kernel, width // heads), shape_of(tok, widt...  12.4 us
    all_to_all x1, waiting for transfers between devices, on_device(): lax.all_to_all(blocks, 'scene', split_axis=1, concat_axis=1, tiled=True)  8.69 us
    all_to_all x1, starting transfers between devices, on_device(): lax.all_to_all(blocks, 'scene', split_axis=1, concat_axis=1, tiled=True)  8.08 us
  transfers between devices with their start and end apart: 7, of which 5 were waited for; matrix products, arithmetic and copies ran while one was open for 3% of the time, Pallas kernels for 0%

commit v1 on v0

--- a/solution.py
+++ b/solution.py
@@ -13,6 +13,7 @@
 TILE = 128
 F32 = jnp.float32
 BF16 = jnp.bfloat16
+MESH = pl.DeviceIdType.MESH
 VMEM_LIMIT = 56 * 1024 * 1024
 
 
@@ -175,6 +176,240 @@
     g = grad_normed[...]
     along = jnp.mean(g * normed, axis=-1, keepdims=True)
     mid_ref[...] = cot + scale * (g - jnp.mean(g, axis=-1, keepdims=True) - normed * along)
+
+
+def bits_of(index, order):
+    return tuple((index >> bit) & 1 for bit in order)
+
+
+def mlp_reduce_kernel(
+    grad_scale, orders_ab, batch_count,
+    first_ref, mixed_ref, cot_ref, up_ref, down_ref,
+    out_ref, mid_ref, gup_ref, gdown_ref,
+    n_left, c_left, nt_left, ct_left, slope, act_hi, act_lo, gh_hi, gh_lo,
+    acc_a, acc_b, recv_a, recv_b, zrecv_a, zsend_b, zrecv_b,
+    send_sem, recv_sem, za_send, za_recv, zb_send, zb_recv,
+):
+    tok, width = first_ref.shape
+    hidden_width = up_ref.shape[1]
+    steps = len(orders_ab[0])
+    scene_count = 2**steps
+    rows_a, rows_b = width // scene_count, hidden_width // scene_count
+    cols_a, cols_b = hidden_width // batch_count, width // batch_count
+    pieces_a, pieces_b = cols_a // TILE, width // TILE
+    me, my_batch = lax.axis_index("scene"), lax.axis_index("batch")
+    values = [(me // 2**bit) % 2 for bit in range(steps)]
+    partners = [me + (1 - 2 * values[bit]) * 2**bit for bit in range(steps)]
+    others = [lax.rem(my_batch + d, batch_count) for d in range(1, batch_count)]
+
+    barrier = pltpu.get_barrier_semaphore()
+    for partner in partners:
+        pl.semaphore_signal(barrier, inc=1, device_id={"scene": partner}, device_id_type=MESH)
+    for other in others:
+        pl.semaphore_signal(barrier, inc=1, device_id={"batch": other}, device_id_type=MESH)
+
+    accs, recvs = (acc_a, acc_b), (recv_a, recv_b)
+    sent = []
+
+    def kept(stream, upto):
+        return tuple(values[bit] for bit in orders_ab[stream][:upto])
+
+    def halving(stream, q, i):
+        bit = orders_ab[stream][i]
+        return pltpu.make_async_remote_copy(
+            src_ref=accs[stream].at[(q, *kept(stream, i), 1 - values[bit])],
+            dst_ref=recvs[stream][i].at[q],
+            send_sem=send_sem.at[stream, q, i],
+            recv_sem=recv_sem.at[stream, q, i],
+            device_id={"scene": partners[bit]},
+            device_id_type=MESH,
+        )
+
+    def start(copy):
+        copy.start()
+        sent.append(copy)
+
+    def z_a(q, d):
+        return pltpu.make_async_remote_copy(
+            src_ref=acc_a.at[(q, *kept(0, steps), others[d])],
+            dst_ref=zrecv_a.at[q, d],
+            send_sem=za_send.at[q, d],
+            recv_sem=za_recv.at[q, d],
+            device_id={"batch": others[d]},
+            device_id_type=MESH,
+        )
+
+    def z_b(d):
+        return pltpu.make_async_remote_copy(
+            src_ref=zsend_b.at[others[d]],
+            dst_ref=zrecv_b.at[d],
+            send_sem=zb_send.at[d],
+            recv_sem=zb_recv.at[d],
+            device_id={"batch": others[d]},
+            device_id_type=MESH,
+        )
+
+    def advance(stream, q, i):
+        halving(stream, q, i).wait_recv()
+        mine = (q, *kept(stream, i + 1))
+        accs[stream][mine] = accs[stream][mine] + recvs[stream][i][q]
+        if i + 1 < steps:
+            start(halving(stream, q, i + 1))
+        elif stream == 0:
+            for d in range(batch_count - 1):
+                start(z_a(q, d))
+        elif q == pieces_b - 1:
+            whole = jnp.concatenate([acc_b[(p, *kept(1, steps))] for p in range(pieces_b)], axis=1)
+            pad = zsend_b.shape[2] - rows_b
+            whole = jnp.concatenate([whole, jnp.zeros((pad, width), F32)], axis=0)
+            zsend_b[...] = whole.T.reshape(zsend_b.shape)
+            for d in range(batch_count - 1):
+                start(z_b(d))
+
+    middle = first_ref[...] + mixed_ref[...]
+    normed, scale = norm_of(middle)
+    cot = cot_ref[...]
+    n_left[...] = left3(normed)
+    c_left[...] = left3(cot)
+    nt_left[...] = left3(normed.T * grad_scale)
+    ct_left[...] = left3(cot.T * grad_scale)
+
+    chunk = 2 * rows_b
+    for c in range(hidden_width // chunk):
+        at = slice(c * chunk, (c + 1) * chunk)
+        hidden = dot(n_left[...], right3(up_ref[:, at]))
+        cdf = 0.5 * (1.0 + lax.erf(hidden * (0.5**0.5)))
+        density = jnp.exp(-0.5 * hidden * hidden) * ((2.0 * np.pi) ** -0.5)
+        slope[:, at] = cdf + hidden * density
+        hi, lo = split(hidden * cdf)
+        act_hi[:, at] = hi
+        act_lo[:, at] = lo
+        grad = dot(ct_left[...], jnp.concatenate([hi, lo, hi], axis=0)).T
+        for half in range(2):
+            block = bits_of(2 * c + half, orders_ab[1])
+            for q in range(pieces_b):
+                acc_b[(q, *block)] = grad[half * rows_b : (half + 1) * rows_b, q * TILE : (q + 1) * TILE]
+
+    pl.semaphore_wait(barrier, steps + batch_count - 1)
+    for q in range(pieces_b):
+        start(halving(1, q, 0))
+
+    part = batch_count * TILE
+    for q in range(pieces_a):
+        where = [slice(b * cols_a + q * TILE, b * cols_a + (q + 1) * TILE) for b in range(batch_count)]
+        down = jnp.concatenate([down_ref[w, :] for w in where], axis=0)
+        grad_act = dot_t(c_left[...], right3(down, axis=1))
+        hi, lo = split(grad_act * jnp.concatenate([slope[:, w] for w in where], axis=1))
+        gh_hi[:, q * part : (q + 1) * part] = hi
+        gh_lo[:, q * part : (q + 1) * part] = lo
+        grad = dot(nt_left[...], jnp.concatenate([hi, lo, hi], axis=0))
+        for s in range(scene_count):
+            for b in range(batch_count):
+                acc_a[(q, *bits_of(s, orders_ab[0]), b)] = grad[
+                    s * rows_a : (s + 1) * rows_a, b * TILE : (b + 1) * TILE
+                ]
+        start(halving(0, q, 0))
+        if q == 0:
+            for p in range(pieces_b):
+                advance(1, p, 0)
+        else:
+            advance(0, q - 1, 0)
+
+    down_hi, down_lo = split(down_ref[...])
+    out_ref[...] = (
+        middle + dot(act_hi[...], down_hi) + dot(act_hi[...], down_lo) + dot(act_lo[...], down_hi)
+    )
+    advance(0, pieces_a - 1, 0)
+    advance(1, 0, 1)
+    advance(0, 0, 1)
+
+    g = jnp.zeros((tok, width), F32)
+    for q in range(pieces_a):
+        where = [slice(b * cols_a + q * TILE, b * cols_a + (q + 1) * TILE) for b in range(batch_count)]
+        up_hi, up_lo = split(jnp.concatenate([up_ref[:, w] for w in where], axis=1))
+        hi, lo = gh_hi[:, q * part : (q + 1) * part], gh_lo[:, q * part : (q + 1) * part]
+        g += dot_t(hi, up_hi) + dot_t(hi, up_lo) + dot_t(lo, up_hi)
+    along = jnp.mean(g * normed, axis=-1, keepdims=True)
+    mid_ref[...] = cot + scale * (g - jnp.mean(g, axis=-1, keepdims=True) - normed * along)
+
+    for i in range(1, steps):
+        for q in range(max(pieces_a, pieces_b)):
+            for stream, count in ((1, pieces_b), (0, pieces_a)):
+                if q < count and not (i == 1 and q == 0):
+                    advance(stream, q, i)
+    for q in range(pieces_a):
+        total = acc_a[(q, *kept(0, steps), my_batch)]
+        for d in range(batch_count - 1):
+            z_a(q, d).wait_recv()
+            total += zrecv_a[q, d]
+        gup_ref[:, q * TILE : (q + 1) * TILE] = total
+    total = zsend_b[my_batch]
+    for d in range(batch_count - 1):
+        z_b(d).wait_recv()
+        total += zrecv_b[d]
+    total = jnp.concatenate([total, jnp.zeros((TILE - cols_b, total.shape[1]), F32)], axis=0)
+    gdown_ref[...] = total.T[:rows_b, :cols_b]
+    for copy in sent:
+        copy.wait_send()
+
+
+def can_fuse(width, hidden_width, scene_count, batch_count):
+    return (
+        scene_count >= 4
+        and scene_count & (scene_count - 1) == 0
+        and batch_count > 1
+        and width % TILE == 0
+        and (width // scene_count) % 8 == 0
+        and (hidden_width // scene_count) % 64 == 0
+        and (hidden_width // batch_count) % TILE == 0
+        and (width // batch_count) % 8 == 0
+        and width // batch_count <= TILE
+    )
+
+
+def mlp_reduced(grad_scale, scene_count, batch_count, first, returned, cot, w_up, w_down):
+    tok, width = first.shape
+    hidden_width = w_up.shape[1]
+    steps = scene_count.bit_length() - 1
+    orders_ab = (tuple(range(steps)), (0, *reversed(range(1, steps))))
+    rows_a, rows_b = width // scene_count, hidden_width // scene_count
+    cols_a, cols_b = hidden_width // batch_count, width // batch_count
+    pieces_a, pieces_b = cols_a // TILE, width // TILE
+    tail_a, tail_b = (batch_count, rows_a, TILE), (rows_b, TILE)
+    padded = -(-rows_b // TILE) * TILE
+    pieces = max(pieces_a, pieces_b)
+    scratch = (
+        [pltpu.VMEM((tok, 3 * width), BF16)] * 2
+        + [pltpu.VMEM((width, 3 * tok), BF16)] * 2
+        + [pltpu.VMEM((tok, hidden_width), F32)]
+        + [pltpu.VMEM((tok, hidden_width), BF16)] * 4
+        + [
+            pltpu.VMEM((pieces_a, *(2,) * steps, *tail_a), F32),
+            pltpu.VMEM((pieces_b, *(2,) * steps, *tail_b), F32),
+            [pltpu.VMEM((pieces_a, *(2,) * (steps - 1 - i), *tail_a), F32) for i in range(steps)],
+            [pltpu.VMEM((pieces_b, *(2,) * (steps - 1 - i), *tail_b), F32) for i in range(steps)],
+            pltpu.VMEM((pieces_a, batch_count - 1, rows_a, TILE), F32),
+            pltpu.VMEM((batch_count, cols_b, padded), F32),
+            pltpu.VMEM((batch_count - 1, cols_b, padded), F32),
+        ]
+        + [pltpu.SemaphoreType.DMA((2, pieces, steps))] * 2
+        + [pltpu.SemaphoreType.DMA((pieces_a, batch_count - 1))] * 2
+        + [pltpu.SemaphoreType.DMA((batch_count - 1,))] * 2
+    )
+    return pl.pallas_call(
+        functools.partial(mlp_reduce_kernel, grad_scale, orders_ab, batch_count),
+        out_shape=(
+            shape_of(tok, width),
+            shape_of(tok, width),
+            shape_of(rows_a, cols_a),
+            shape_of(rows_b, cols_b),
+        ),
+        scratch_shapes=scratch,
+        compiler_params=pltpu.CompilerParams(
+            vmem_limit_bytes=VMEM_LIMIT, collective_id=0, has_side_effects=True
+        ),
+        cost_estimate=pl.CostEstimate(flops=10**10, bytes_accessed=4000000, transcendentals=0),
+    )(first, returned, cot, w_up, w_down)
 
 
 def shape_of(*dims):
@@ -240,6 +475,11 @@
         mixed.reshape(per, scene_count, count, width), "scene", split_axis=1, concat_axis=1, tiled=True
     ).reshape(tok, width)
     grad_scale = float(tok * scene_count * batch_count) ** -0.5
+    if can_fuse(width, hidden_width, scene_count, batch_count):
+        block_out, grad_mid, *grads = mlp_reduced(
+            grad_scale, scene_count, batch_count, first, returned, cotangent[0], w_up, w_down
+        )
+        return (block_out[None], grad_mid[None], *grads)
     block_out, grad_mid, grad_up, grad_down = call(
         functools.partial(mlp_kernel, grad_scale),
         (

time: 229 us -> 120 us (0.52)
  waiting for transfers between devices: 137 us -> 8.75 us
  Pallas kernels: 38.1 us -> 69 us
  between operations: 13.8 us -> 0.74 us
    reduce_scatter x3 -> x0, waiting for transfers between devices: 105 us -> none  [the longest x2 85.5 us: on_device(): part = lax.psum_scatter(grad, 'scene', scatter_dimension=0, tiled=True)]
    pallas_call x1, Pallas kernels: 17.9 us -> 48.9 us  [mlp_reduced(): pl.pallas_call(functools.partial(mlp_reduce_kernel, grad_scale, orders_ab...]
    unnamed x5 -> x0, waiting for transfers between devices: 23.6 us -> none
    unnamed x9 -> x15, local copies, waits for them, and re-layouts: 5.58 us -> 7.22 us
  transfers between devices with their start and end apart: 7 -> 3, of which waited for: 5 -> 1; matrix products, arithmetic and copies ran while one was open for 3% -> 3% of each run, Pallas kernels for 0% -> 0%
where the time goes in v1:
time: 120 us; the launch traced here: 119 us
  Pallas kernels  69 us (58%)
  local copies, waits for them, and re-layouts  15.7 us (13%)
  blocking collectives  12.8 us (11%)
  starting transfers between devices  12.4 us (10%)
  waiting for transfers between devices  8.75 us (7%)
    pallas_call x1, Pallas kernels, mlp_reduced(): pl.pallas_call(functools.partial(mlp_reduce_kernel, grad_scale, orders_ab...  48.9 us
    all_to_all x1, blocking collectives, on_device(): lax.all_to_all(mixed.reshape(per, scene_count, count, width), 'scene', sp...  12.8 us
    pallas_call x1, Pallas kernels, on_device(): call(functools.partial(attend_kernel, width // heads), shape_of(tok, widt...  12.4 us
    all_to_all x1, waiting for transfers between devices, on_device(): lax.all_to_all(blocks, 'scene', split_axis=1, concat_axis=1, tiled=True)  8.74 us
    all_to_all x1, starting transfers between devices, on_device(): lax.all_to_all(blocks, 'scene', split_axis=1, concat_axis=1, tiled=True)  8.08 us
    pallas_call x1, Pallas kernels, on_device(): call(conv_kernel, (shape_of(tok, width), shape_of(tok, width)), [pltpu.VM...  7.75 us
    unnamed x15, local copies, waits for them, and re-layouts  7.22 us
    ppermute x1, starting transfers between devices, on_device(): low = lax.ppermute(local[tok - HALO:], 'scene', forward)  3.04 us
  transfers between devices with their start and end apart: 3, of which 1 were waited for; matrix products, arithmetic and copies ran while one was open for 3% of the time, Pallas kernels for 0%

profile of v1, /device:TPU:0, one launch (start us, length us, event | category | flops | bytes accessed | tf_op | source)
XLA Modules:
  0.0 119.4 jit_solution(14815656774306251982)
XLA Ops:
  0.6 1.0 slice_bitcast_fusion
  1.6 1.3 %collective-permute-start.1 = (f32[64,384]{1,0:T(8,128)S(1)}, f32[64,384]{1,0:T(8,128)S(1)}, u32[]{:S(2)}, u32[]{:S(2)}) collective-permute-start(f32[64,384]{1,0:T(8,128)S(1)} %get-tuple-element.16), channel_id=1, source_target_pairs={{4,0},{8,4},{12,8},{16,12},{20,16},{24,20},{28,24},{5,1},{9,5},{13... | collective-permute-start | bytes 294920 | tf_op jit(solution)/shard_map/ppermute | solution.py:449
  2.9 3.0 %collective-permute-start = (f32[64,384]{1,0:T(8,128)S(1)}, f32[64,384]{1,0:T(8,128)S(1)}, u32[]{:S(2)}, u32[]{:S(2)}) collective-permute-start(f32[64,384]{1,0:T(8,128)S(1)} %get-tuple-element.17), channel_id=1, source_target_pairs={{0,4},{4,8},{8,12},{12,16},{16,20},{20,24},{24,28},{1,5},{5,9},{9,... | collective-permute-start | bytes 294920 | tf_op jit(solution)/shard_map/ppermute | solution.py:448
  5.9 1.4 %copy.21 = s32[27,1,384]{2,0,1:T(8,128)} copy(s32[27,1,384]{2,1,0:T(1,128)} %param.12) | data formatting | bytes 82944
  7.4 0.6 copy-done.3
  8.0 7.7 %shard_map.138 = (f32[384,384]{1,0:T(8,128)}, f32[384,384]{1,0:T(8,128)}) custom-call(f32[384,384]{1,0:T(8,128)} %bitcast.13, f32[64,384]{1,0:T(8,128)} %copy-done.4, f32[64,384]{1,0:T(8,128)} %copy-done.3, s32[27,384]{1,0:T(8,128)} %bitcast.14, f32[27,384]{1,0:T(8,128)} %weight_ref.1), custom_call_target="tpu_custom_call" | custom-call | flops 8000000000 | bytes 4000000 | tf_op jit(solution)/shard_map/pallas_call | solution.py:450
  15.8 1.2 reshape.26
  16.9 1.2 %copy.15 = f32[4,8,12,384]{3,0,2,1:T(4,128)} copy(f32[4,8,12,384]{3,2,1,0:T(8,128)S(1)} %reshape.26) | data formatting | bytes 1179648 | tf_op jit(solution)/shard_map/reshape | solution.py:457
  18.1 8.1 %all-to-all-start = ((f32[4,8,12,384]{3,0,2,1:T(4,128)}), f32[4,8,12,384]{3,0,2,1:T(4,128)S(1)}, u32[]{:S(2)}, u32[]{:S(2)}) async-start(f32[4,8,12,384]{3,0,2,1:T(4,128)} %copy.15), calls=%async_computation | async-start | bytes 1179648 | tf_op jit(solution)/shard_map/all_to_all | solution.py:458
  26.2 0.3 tile.4
  26.5 1.4 %tile.10.bias_ref = f32[24,32,128]{2,1,0:T(8,128)} reshape(f32[24,32,4,32]{3,2,1,0:T(4,128)S(1)} %tile.4) | data formatting | bytes 786432 | tf_op jit(solution)/shard_map/tile | solution.py:460
  27.9 8.7 %all-to-all-done = f32[4,8,12,384]{3,0,2,1:T(4,128)S(1)} async-done(((f32[4,8,12,384]{3,0,2,1:T(4,128)}), f32[4,8,12,384]{3,0,2,1:T(4,128)S(1)}, u32[]{:S(2)}, u32[]{:S(2)}) %all-to-all-start) | async-done | bytes 589856 | tf_op jit(solution)/shard_map/all_to_all | solution.py:458
  36.7 0.1 copy.16
  36.8 0.9 reshape.27.x_ref
  37.6 12.4 %shard_map.139 = f32[384,384]{1,0:T(8,128)} custom-call(f32[384,384]{1,0:T(8,128)} %reshape.27.x_ref, bf16[384,384]{1,0:T(8,128)(2,1)} %constant.4.clone.perm_ref, bf16[384,384]{1,0:T(8,128)(2,1)} %constant.5.clone.back_ref, f32[384,1152]{1,0:T(8,128)} %wqkv_ref.1, f32[384,384]{1,0:T(8,128)} %wout_ref.1, f32[24,32,128]{2,1,0:T(8,128)} %tile.10.bias_ref), custom_call_target="tpu_custom_call" | custom-call | flops 10000000000 | bytes 4000000 | tf_op jit(solution)/shard_map/pallas_call | solution.py:461
  50.0 1.1 reshape.28
  51.2 0.4 copy.17
  51.6 12.8 %all_to_all.10 = f32[4,8,12,384]{3,0,2,1:T(4,128)S(1)} all-to-all(f32[4,8,12,384]{3,0,2,1:T(4,128)S(1)} %copy.17), channel_id=1, replica_groups=mesh['scene'=8,'batch'=4] {'scene'}, dimensions={1} | all-to-all | bytes 1179648 | tf_op jit(solution)/shard_map/all_to_all | solution.py:474
  64.5 0.9 reshape.29.mixed_ref
  65.3 48.9 %shard_map.140 = (f32[384,384]{1,0:T(8,128)}, f32[384,384]{1,0:T(8,128)}, f32[48,384]{1,0:T(8,128)}, f32[192,96]{1,0:T(8,128)}) custom-call(f32[384,384]{1,0:T(8,128)} %get-tuple-element.10.first_ref, f32[384,384]{1,0:T(8,128)} %reshape.29.mixed_ref, f32[384,384]{1,0:T(8,128)} %bitcast.15, f32[384,1536]{1,0:T(8,128)} %up_ref.1, f32[1536,384]{1,0:T(8,128)} %down_ref.1), custom_call_target="tpu_custom_call" | custom-call | flops 10000000000 | bytes 4000000 | tf_op jit(solution)/shard_map/pallas_call | solution.py:399
  114.3 2.0 %copy.26 = f32[1,384,384]{2,1,0:T(8,128)} copy(f32[1,384,384]{2,1,0:T(8,128)} %bitcast.12) | data formatting | bytes 1179648
  116.2 1.9 %copy.27 = f32[1,384,384]{2,1,0:T(8,128)} copy(f32[1,384,384]{2,1,0:T(8,128)} %bitcast.11) | data formatting | bytes 1179648
  118.1 0.6 copy.28
  118.8 0.6 copy.29
  (12 shorter events, 0.1 us)
Async XLA Ops:
  1.6 5.8 %collective-permute-start.1 = (f32[64,384]{1,0:T(8,128)S(1)}, f32[64,384]{1,0:T(8,128)S(1)}, u32[]{:S(2)}, u32[]{:S(2)}) collective-permute-start(f32[64,384]{1,0:T(8,128)S(1)} %get-tuple-element.16), channel_id=1, source_target_pairs={{4,0},{8,4},{12,8},{16,12},{20,16},{24,20},{28,24},{5,1},{9,5},{13... | collective-permute-start | bytes 294920 | tf_op jit(solution)/shard_map/ppermute | solution.py:449
  2.9 4.5 %collective-permute-start = (f32[64,384]{1,0:T(8,128)S(1)}, f32[64,384]{1,0:T(8,128)S(1)}, u32[]{:S(2)}, u32[]{:S(2)}) collective-permute-start(f32[64,384]{1,0:T(8,128)S(1)} %get-tuple-element.17), channel_id=1, source_target_pairs={{0,4},{4,8},{8,12},{12,16},{16,20},{20,24},{24,28},{1,5},{5,9},{9,... | collective-permute-start | bytes 294920 | tf_op jit(solution)/shard_map/ppermute | solution.py:448
  7.3 0.6 copy-start.3
  7.4 0.7 copy-start.4
  15.8 10.5 %copy-start = (f32[24,32,32]{2,1,0:T(8,128)S(1)}, f32[24,32,32]{2,1,0:T(8,128)}, u32[]{:S(2)}) copy-start(f32[24,32,32]{2,1,0:T(8,128)} %param.17) | copy-start | bytes 294916
  18.1 18.5 %all-to-all-start = ((f32[4,8,12,384]{3,0,2,1:T(4,128)}), f32[4,8,12,384]{3,0,2,1:T(4,128)S(1)}, u32[]{:S(2)}, u32[]{:S(2)}) async-start(f32[4,8,12,384]{3,0,2,1:T(4,128)} %copy.15), calls=%async_computation | async-start | bytes 1179648 | tf_op jit(solution)/shard_map/all_to_all | solution.py:458
  114.2 3.9 %copy-start.2 = (f32[48,384]{1,0:T(8,128)S(1)}, f32[48,384]{1,0:T(8,128)}, u32[]{:S(2)}) copy-start(f32[48,384]{1,0:T(8,128)} %get-tuple-element.24) | copy-start | bytes 221188
  114.2 4.5 %copy-start.1 = (f32[192,96]{1,0:T(8,128)S(1)}, f32[192,96]{1,0:T(8,128)}, u32[]{:S(2)}) copy-start(f32[192,96]{1,0:T(8,128)} %get-tuple-element.25) | copy-start | bytes 221188

commit v2 on v1

--- a/solution.py
+++ b/solution.py
@@ -182,69 +182,230 @@
     return tuple((index >> bit) & 1 for bit in order)
 
 
-def mlp_reduce_kernel(
-    grad_scale, orders_ab, batch_count,
-    first_ref, mixed_ref, cot_ref, up_ref, down_ref,
+def block_kernel(
+    grad_scale, orders_ab, batch_count, head_dim,
+    local_ref, offset_ref, weight_ref, up_hbm, down_hbm, qkv_hbm, wout_hbm, cot_hbm, bias_ref,
+    spread_ref, gather_ref, slots_ref, unslots_ref,
     out_ref, mid_ref, gup_ref, gdown_ref,
+    up_ref, down_ref, wqkv_ref, wout_ref, cot_ref, load_sem,
+    low, high, halo_send, halo_recv, ext, off_t, first_ref,
+    x_send, x_recv, y_send, y_recv, xs_sem, xr_sem, ys_sem, yr_sem,
+    wqkv3, wout3, bias_tile, up_hi, up_lo, down_hi, down_lo,
     n_left, c_left, nt_left, ct_left, slope, act_hi, act_lo, gh_hi, gh_lo,
     acc_a, acc_b, recv_a, recv_b, zrecv_a, zsend_b, zrecv_b,
     send_sem, recv_sem, za_send, za_recv, zb_send, zb_recv,
 ):
-    tok, width = first_ref.shape
+    tok, width = local_ref.shape
     hidden_width = up_ref.shape[1]
     steps = len(orders_ab[0])
     scene_count = 2**steps
     rows_a, rows_b = width // scene_count, hidden_width // scene_count
     cols_a, cols_b = hidden_width // batch_count, width // batch_count
     pieces_a, pieces_b = cols_a // TILE, width // TILE
+    tiles = tok // TILE
     me, my_batch = lax.axis_index("scene"), lax.axis_index("batch")
     values = [(me // 2**bit) % 2 for bit in range(steps)]
     partners = [me + (1 - 2 * values[bit]) * 2**bit for bit in range(steps)]
     others = [lax.rem(my_batch + d, batch_count) for d in range(1, batch_count)]
+    scenes = [lax.rem(me + d, scene_count) for d in range(1, scene_count)]
 
     barrier = pltpu.get_barrier_semaphore()
-    for partner in partners:
-        pl.semaphore_signal(barrier, inc=1, device_id={"scene": partner}, device_id_type=MESH)
+    for other in scenes:
+        pl.semaphore_signal(barrier, inc=1, device_id={"scene": other}, device_id_type=MESH)
     for other in others:
         pl.semaphore_signal(barrier, inc=1, device_id={"batch": other}, device_id_type=MESH)
-
-    accs, recvs = (acc_a, acc_b), (recv_a, recv_b)
+    loads = [
+        pltpu.make_async_copy(source, target, load_sem.at[i])
+        for i, (source, target) in enumerate(
+            (
+                (qkv_hbm, wqkv_ref),
+                (wout_hbm, wout_ref),
+                (cot_hbm, cot_ref),
+                (up_hbm, up_ref),
+                (down_hbm, down_ref),
+            )
+        )
+    ]
+    for load in loads:
+        load.start()
+
     sent = []
-
-    def kept(stream, upto):
-        return tuple(values[bit] for bit in orders_ab[stream][:upto])
-
-    def halving(stream, q, i):
-        bit = orders_ab[stream][i]
-        return pltpu.make_async_remote_copy(
-            src_ref=accs[stream].at[(q, *kept(stream, i), 1 - values[bit])],
-            dst_ref=recvs[stream][i].at[q],
-            send_sem=send_sem.at[stream, q, i],
-            recv_sem=recv_sem.at[stream, q, i],
-            device_id={"scene": partners[bit]},
-            device_id_type=MESH,
-        )
 
     def start(copy):
         copy.start()
         sent.append(copy)
 
-    def z_a(q, d):
+    def to_scene(source, target, send, recv, other):
         return pltpu.make_async_remote_copy(
-            src_ref=acc_a.at[(q, *kept(0, steps), others[d])],
-            dst_ref=zrecv_a.at[q, d],
-            send_sem=za_send.at[q, d],
-            recv_sem=za_recv.at[q, d],
-            device_id={"batch": others[d]},
+            src_ref=source,
+            dst_ref=target,
+            send_sem=send,
+            recv_sem=recv,
+            device_id={"scene": other},
             device_id_type=MESH,
         )
 
-    def z_b(d):
+    halo = [
+        to_scene(local_ref.at[pl.ds(tok - HALO, HALO)], low, halo_send.at[0], halo_recv.at[0], scenes[0]),
+        to_scene(local_ref.at[pl.ds(0, HALO)], high, halo_send.at[1], halo_recv.at[1], scenes[-1]),
+    ]
+    pl.semaphore_wait(barrier, scene_count + batch_count - 2)
+    for copy in halo:
+        start(copy)
+
+    taps = weight_ref.shape[0]
+    span = TILE + 2 * HALO
+
+    def extend(row, block):
+        hi, lo = split(block)
+        ext[pl.ds(row, block.shape[0]), :width] = hi
+        ext[pl.ds(row, block.shape[0]), width:] = lo
+
+    extend(HALO, local_ref[...])
+    for t in range(tiles):
+        piece = offset_ref[:, t * TILE : (t + 1) * TILE]
+        piece = jnp.where(piece > HALO, 4 * TILE, piece).astype(F32)
+        piece = jnp.concatenate([piece, jnp.zeros((TILE - taps, TILE), F32)], axis=0)
+        off_t[t * TILE : (t + 1) * TILE, :] = piece.T
+    base = (
+        lax.broadcasted_iota(jnp.int32, (TILE, span), 1)
+        - lax.broadcasted_iota(jnp.int32, (TILE, span), 0)
+        - HALO
+    ).astype(F32)
+
+    def convolve(t):
+        row = pl.multiple_of(t * TILE, TILE)
+        window = ext[pl.ds(row, span), :]
+        offsets = off_t[pl.ds(row, TILE), :]
+        total = local_ref[pl.ds(row, TILE), :]
+        for a in range(taps):
+            pick = jnp.where(base == offsets[:, a : a + 1], 1.0, 0.0).astype(BF16)
+            found = dot(pick, window)
+            total += (found[:, :width] + found[:, width:]) * weight_ref[a : a + 1, :]
+        first_ref[pl.ds(row, TILE), :] = total
+
+    pl.loop(1, tiles - 1)(convolve)
+    for copy in halo:
+        copy.wait_recv()
+    extend(0, jnp.where(me == 0, 0.0, low[...]))
+    extend(HALO + tok, jnp.where(me == scene_count - 1, 0.0, high[...]))
+    pl.loop(0, 2)(lambda j: convolve(j * (tiles - 1)))
+
+    def move(matrix, rows):
+        hi, lo = split(rows)
+        return dot(matrix, hi), dot(matrix, lo)
+
+    piece_rows = TILE // scene_count
+    hi, lo = move(spread_ref[...], norm_of(first_ref[...])[0])
+    x_send[...] = (hi + lo).reshape(x_send.shape)
+
+    def exchange(source, target, t, d, send, recv):
+        return to_scene(
+            source.at[t, scenes[d]], target.at[t, me], send.at[t, d], recv.at[t, d], scenes[d]
+        )
+
+    for t in range(tiles):
+        for d in range(scene_count - 1):
+            start(exchange(x_send, x_recv, t, d, xs_sem, xr_sem))
+        x_recv[t, me] = x_send[t, me]
+
+    loads[0].wait()
+    for part in range(3):
+        at = slice(part * width, (part + 1) * width)
+        wqkv3[:, at] = right3(wqkv_ref[:, at])
+    loads[1].wait()
+    wout3[...] = right3(wout_ref[...])
+    for h in range(bias_ref.shape[0]):
+        bias_tile[h] = jnp.concatenate([bias_ref[h]] * (TILE // GROUP), axis=1)
+    shape = (TILE, TILE)
+    same = (lax.broadcasted_iota(jnp.int32, shape, 0) ^ lax.broadcasted_iota(jnp.int32, shape, 1)) < GROUP
+    away = jnp.where(same, 0.0, -1e30)
+    lane = lax.broadcasted_iota(jnp.int32, shape, 1)
+    per_lane = TILE // head_dim
+
+    def attend(qkv, part):
+        at = part * TILE
+        q = qkv[:, at : at + TILE] * (head_dim**-0.5)
+        k = qkv[:, width + at : width + at + TILE]
+        v = qkv[:, 2 * width + at : 2 * width + at + TILE]
+        keys, vals = [], []
+        for h in range(per_lane):
+            mine = (lane >= h * head_dim) & (lane < (h + 1) * head_dim)
+            keys.append(right3(jnp.where(mine, k, 0.0), axis=1))
+            vals.append(jnp.concatenate(split(jnp.where(mine, v, 0.0)), axis=1))
+        scores = dot_t(left3(q), jnp.concatenate(keys, axis=0))
+        his, los = [], []
+        for h in range(per_lane):
+            bias = jnp.concatenate([bias_tile[part * per_lane + h]] * (TILE // GROUP), axis=0)
+            s = scores[:, h * TILE : (h + 1) * TILE] + bias + away
+            e = jnp.exp(s - jnp.max(s, axis=-1, keepdims=True))
+            p_hi, p_lo = split(e / jnp.sum(e, axis=-1, keepdims=True))
+            his.append(p_hi)
+            los.append(p_lo)
+        vals = jnp.concatenate(vals, axis=0)
+        both = dot(jnp.concatenate(his, axis=1), vals)
+        rest = dot(jnp.concatenate(los, axis=1), vals[:, :TILE])
+        return both[:, :TILE] + both[:, TILE:] + rest
+
+    for t in range(tiles):
+        for d in range(scene_count - 1):
+            exchange(x_send, x_recv, t, d, xs_sem, xr_sem).wait_recv()
+        hi, lo = move(slots_ref[...], x_recv[t].reshape(TILE, width))
+        hi, lo = hi.astype(BF16), lo.astype(BF16)
+        qkv = dot(jnp.concatenate([hi, hi, lo], axis=1), wqkv3[...])
+        att = jnp.concatenate([attend(qkv, part) for part in range(width // TILE)], axis=1)
+        hi, lo = move(unslots_ref[...], att)
+        hi, lo = hi.astype(BF16), lo.astype(BF16)
+        mixed = dot(jnp.concatenate([hi, hi, lo], axis=1), wout3[...])
+        y_send[t] = mixed.reshape(scene_count, piece_rows, width)
+        for d in range(scene_count - 1):
+            start(exchange(y_send, y_recv, t, d, ys_sem, yr_sem))
+        y_recv[t, me] = y_send[t, me]
+
+    loads[2].wait()
+    cot = cot_ref[...]
+    c_left[...] = left3(cot)
+    cot_t = cot.T * grad_scale
+    sub = TILE // batch_count
+    ct_left[...] = left3(
+        jnp.concatenate(
+            [
+                cot_t[b * cols_b + q * sub : b * cols_b + (q + 1) * sub]
+                for q in range(pieces_b)
+                for b in range(batch_count)
+            ],
+            axis=0,
+        )
+    )
+    for load, source, hi_ref, lo_ref in ((loads[3], up_ref, up_hi, up_lo), (loads[4], down_ref, down_hi, down_lo)):
+        load.wait()
+        hi, lo = split(source[...])
+        hi_ref[...] = hi
+        lo_ref[...] = lo
+
+    accs, recvs = (acc_a, acc_b), (recv_a, recv_b)
+
+    def kept(stream, upto):
+        return tuple(values[bit] for bit in orders_ab[stream][:upto])
+
+    def halving(stream, q, i):
+        bit = orders_ab[stream][i]
+        return to_scene(
+            accs[stream].at[(q, *kept(stream, i), 1 - values[bit])],
+            recvs[stream][i].at[q],
+            send_sem.at[stream, q, i],
+            recv_sem.at[stream, q, i],
+            partners[bit],
+        )
+
+    def to_batch(stream, q, d):
+        send, recv = ((za_send, za_recv), (zb_send, zb_recv))[stream]
+        source = acc_a.at[(q, *kept(0, steps), others[d])] if stream == 0 else zsend_b.at[q, others[d]]
         return pltpu.make_async_remote_copy(
-            src_ref=zsend_b.at[others[d]],
-            dst_ref=zrecv_b.at[d],
-            send_sem=zb_send.at[d],
-            recv_sem=zb_recv.at[d],
+            src_ref=source,
+            dst_ref=(zrecv_a, zrecv_b)[stream].at[q, d],
+            send_sem=send.at[q, d],
+            recv_sem=recv.at[q, d],
             device_id={"batch": others[d]},
             device_id_type=MESH,
         )
@@ -255,29 +416,26 @@
         accs[stream][mine] = accs[stream][mine] + recvs[stream][i][q]
         if i + 1 < steps:
             start(halving(stream, q, i + 1))
-        elif stream == 0:
-            for d in range(batch_count - 1):
-                start(z_a(q, d))
-        elif q == pieces_b - 1:
-            whole = jnp.concatenate([acc_b[(p, *kept(1, steps))] for p in range(pieces_b)], axis=1)
-            pad = zsend_b.shape[2] - rows_b
-            whole = jnp.concatenate([whole, jnp.zeros((pad, width), F32)], axis=0)
-            zsend_b[...] = whole.T.reshape(zsend_b.shape)
-            for d in range(batch_count - 1):
-                start(z_b(d))
-
-    middle = first_ref[...] + mixed_ref[...]
+            return
+        if stream == 1:
+            pad = jnp.zeros((zsend_b.shape[-1] - rows_b, TILE), F32)
+            whole = jnp.concatenate([acc_b[mine], pad], axis=0)
+            zsend_b[q] = whole.T.reshape(zsend_b.shape[1:])
+        for d in range(batch_count - 1):
+            start(to_batch(stream, q, d))
+
+    for t in range(tiles):
+        for d in range(scene_count - 1):
+            exchange(y_send, y_recv, t, d, ys_sem, yr_sem).wait_recv()
+    hi, lo = move(gather_ref[...], y_recv[...].reshape(tok, width))
+    middle = first_ref[...] + (hi + lo)
     normed, scale = norm_of(middle)
-    cot = cot_ref[...]
     n_left[...] = left3(normed)
-    c_left[...] = left3(cot)
-    nt_left[...] = left3(normed.T * grad_scale)
-    ct_left[...] = left3(cot.T * grad_scale)
 
     chunk = 2 * rows_b
     for c in range(hidden_width // chunk):
         at = slice(c * chunk, (c + 1) * chunk)
-        hidden = dot(n_left[...], right3(up_ref[:, at]))
+        hidden = dot(n_left[...], jnp.concatenate([up_hi[:, at], up_lo[:, at], up_hi[:, at]], axis=0))
         cdf = 0.5 * (1.0 + lax.erf(hidden * (0.5**0.5)))
         density = jnp.exp(-0.5 * hidden * hidden) * ((2.0 * np.pi) ** -0.5)
         slope[:, at] = cdf + hidden * density
@@ -289,17 +447,20 @@
             block = bits_of(2 * c + half, orders_ab[1])
             for q in range(pieces_b):
                 acc_b[(q, *block)] = grad[half * rows_b : (half + 1) * rows_b, q * TILE : (q + 1) * TILE]
-
-    pl.semaphore_wait(barrier, steps + batch_count - 1)
     for q in range(pieces_b):
         start(halving(1, q, 0))
+    nt_left[...] = left3(normed.T * grad_scale)
 
     part = batch_count * TILE
+    wheres = [
+        [slice(b * cols_a + q * TILE, b * cols_a + (q + 1) * TILE) for b in range(batch_count)]
+        for q in range(pieces_a)
+    ]
     for q in range(pieces_a):
-        where = [slice(b * cols_a + q * TILE, b * cols_a + (q + 1) * TILE) for b in range(batch_count)]
-        down = jnp.concatenate([down_ref[w, :] for w in where], axis=0)
-        grad_act = dot_t(c_left[...], right3(down, axis=1))
-        hi, lo = split(grad_act * jnp.concatenate([slope[:, w] for w in where], axis=1))
+        d_hi = jnp.concatenate([down_hi[w, :] for w in wheres[q]], axis=0)
+        d_lo = jnp.concatenate([down_lo[w, :] for w in wheres[q]], axis=0)
+        grad_act = dot_t(c_left[...], jnp.concatenate([d_hi, d_lo, d_hi], axis=1))
+        hi, lo = split(grad_act * jnp.concatenate([slope[:, w] for w in wheres[q]], axis=1))
         gh_hi[:, q * part : (q + 1) * part] = hi
         gh_lo[:, q * part : (q + 1) * part] = lo
         grad = dot(nt_left[...], jnp.concatenate([hi, lo, hi], axis=0))
@@ -315,9 +476,11 @@
         else:
             advance(0, q - 1, 0)
 
-    down_hi, down_lo = split(down_ref[...])
     out_ref[...] = (
-        middle + dot(act_hi[...], down_hi) + dot(act_hi[...], down_lo) + dot(act_lo[...], down_hi)
+        middle
+        + dot(act_hi[...], down_hi[...])
+        + dot(act_hi[...], down_lo[...])
+        + dot(act_lo[...], down_hi[...])
     )
     advance(0, pieces_a - 1, 0)
     advance(1, 0, 1)
@@ -325,61 +488,105 @@
 
     g = jnp.zeros((tok, width), F32)
     for q in range(pieces_a):
-        where = [slice(b * cols_a + q * TILE, b * cols_a + (q + 1) * TILE) for b in range(batch_count)]
-        up_hi, up_lo = split(jnp.concatenate([up_ref[:, w] for w in where], axis=1))
+        u_hi = jnp.concatenate([up_hi[:, w] for w in wheres[q]], axis=1)
+        u_lo = jnp.concatenate([up_lo[:, w] for w in wheres[q]], axis=1)
         hi, lo = gh_hi[:, q * part : (q + 1) * part], gh_lo[:, q * part : (q + 1) * part]
-        g += dot_t(hi, up_hi) + dot_t(hi, up_lo) + dot_t(lo, up_hi)
+        g += dot_t(hi, u_hi) + dot_t(hi, u_lo) + dot_t(lo, u_hi)
     along = jnp.mean(g * normed, axis=-1, keepdims=True)
-    mid_ref[...] = cot + scale * (g - jnp.mean(g, axis=-1, keepdims=True) - normed * along)
+    mid_ref[...] = cot_ref[...] + scale * (g - jnp.mean(g, axis=-1, keepdims=True) - normed * along)
 
     for i in range(1, steps):
         for q in range(max(pieces_a, pieces_b)):
             for stream, count in ((1, pieces_b), (0, pieces_a)):
                 if q < count and not (i == 1 and q == 0):
                     advance(stream, q, i)
+    rows = []
+    for q in range(pieces_b):
+        total = zsend_b[q, my_batch]
+        for d in range(batch_count - 1):
+            to_batch(1, q, d).wait_recv()
+            total += zrecv_b[q, d]
+        rows.append(total)
+    rows.append(jnp.zeros((TILE - cols_b, rows[0].shape[1]), F32))
+    gdown_ref[...] = jnp.concatenate(rows, axis=0).T[:rows_b, :cols_b]
     for q in range(pieces_a):
         total = acc_a[(q, *kept(0, steps), my_batch)]
         for d in range(batch_count - 1):
-            z_a(q, d).wait_recv()
+            to_batch(0, q, d).wait_recv()
             total += zrecv_a[q, d]
         gup_ref[:, q * TILE : (q + 1) * TILE] = total
-    total = zsend_b[my_batch]
-    for d in range(batch_count - 1):
-        z_b(d).wait_recv()
-        total += zrecv_b[d]
-    total = jnp.concatenate([total, jnp.zeros((TILE - cols_b, total.shape[1]), F32)], axis=0)
-    gdown_ref[...] = total.T[:rows_b, :cols_b]
     for copy in sent:
         copy.wait_send()
 
 
-def can_fuse(width, hidden_width, scene_count, batch_count):
+def can_fuse(tok, width, head_dim, taps, hidden_width, scene_count, batch_count):
     return (
         scene_count >= 4
         and scene_count & (scene_count - 1) == 0
+        and GROUP % scene_count == 0
+        and (TILE // scene_count) % 8 == 0
         and batch_count > 1
+        and tok % TILE == 0
+        and tok // TILE > 1
         and width % TILE == 0
+        and TILE % head_dim == 0
+        and taps <= TILE
+        and TILE % (8 * batch_count) == 0
         and (width // scene_count) % 8 == 0
         and (hidden_width // scene_count) % 64 == 0
         and (hidden_width // batch_count) % TILE == 0
-        and (width // batch_count) % 8 == 0
-        and width // batch_count <= TILE
+        and width // batch_count < TILE
     )
 
 
-def mlp_reduced(grad_scale, scene_count, batch_count, first, returned, cot, w_up, w_down):
-    tok, width = first.shape
+def piece_orders(tok, scene_count):
+    per, count, some = GROUP // scene_count, tok // GROUP, TILE // GROUP
+    row = np.arange(tok)
+    tile, rest = row // TILE, row % TILE
+    device, k, g = rest // (per * some), rest // some % per, rest % some
+    spread = np.zeros((tok, tok), np.float32)
+    spread[row, (k * scene_count + device) * count + tile * some + g] = 1.0
+    row = np.arange(TILE)
+    slots = np.zeros((TILE, TILE), np.float32)
+    slots[row, row % GROUP * some + row // GROUP] = 1.0
+    return spread, slots
+
+
+def fused(scene_count, batch_count, local, offsets, cot, conv_weight, w_qkv, w_out, score_bias, w_up, w_down):
+    tok, width = local.shape
     hidden_width = w_up.shape[1]
+    heads = score_bias.shape[0]
     steps = scene_count.bit_length() - 1
     orders_ab = (tuple(range(steps)), (0, *reversed(range(1, steps))))
     rows_a, rows_b = width // scene_count, hidden_width // scene_count
-    cols_a, cols_b = hidden_width // batch_count, width // batch_count
+    cols_a = hidden_width // batch_count
+    cols_b = width // batch_count
     pieces_a, pieces_b = cols_a // TILE, width // TILE
     tail_a, tail_b = (batch_count, rows_a, TILE), (rows_b, TILE)
     padded = -(-rows_b // TILE) * TILE
-    pieces = max(pieces_a, pieces_b)
+    sub = TILE // batch_count
+    tiles = tok // TILE
+    sems = pltpu.SemaphoreType.DMA
     scratch = (
-        [pltpu.VMEM((tok, 3 * width), BF16)] * 2
+        [pltpu.VMEM(x.shape, F32) for x in (w_up, w_down, w_qkv, w_out, cot)]
+        + [sems((5,))]
+        + [pltpu.VMEM((HALO, width), F32)] * 2
+        + [sems((2,))] * 2
+        + [
+            pltpu.VMEM((tok + 2 * HALO, 2 * width), BF16),
+            pltpu.VMEM((tok, TILE), F32),
+            pltpu.VMEM((tok, width), F32),
+        ]
+        + [pltpu.VMEM((tiles, scene_count, TILE // scene_count, width), F32)] * 4
+        + [sems((tiles, scene_count - 1))] * 4
+        + [
+            pltpu.VMEM((3 * width, 3 * width), BF16),
+            pltpu.VMEM((3 * width, width), BF16),
+            pltpu.VMEM((heads, GROUP, TILE), F32),
+        ]
+        + [pltpu.VMEM(w_up.shape, BF16)] * 2
+        + [pltpu.VMEM(w_down.shape, BF16)] * 2
+        + [pltpu.VMEM((tok, 3 * width), BF16)] * 2
         + [pltpu.VMEM((width, 3 * tok), BF16)] * 2
         + [pltpu.VMEM((tok, hidden_width), F32)]
         + [pltpu.VMEM((tok, hidden_width), BF16)] * 4
@@ -389,15 +596,20 @@
             [pltpu.VMEM((pieces_a, *(2,) * (steps - 1 - i), *tail_a), F32) for i in range(steps)],
             [pltpu.VMEM((pieces_b, *(2,) * (steps - 1 - i), *tail_b), F32) for i in range(steps)],
             pltpu.VMEM((pieces_a, batch_count - 1, rows_a, TILE), F32),
-            pltpu.VMEM((batch_count, cols_b, padded), F32),
-            pltpu.VMEM((batch_count - 1, cols_b, padded), F32),
+            pltpu.VMEM((pieces_b, batch_count, sub, padded), F32),
+            pltpu.VMEM((pieces_b, batch_count - 1, sub, padded), F32),
         ]
-        + [pltpu.SemaphoreType.DMA((2, pieces, steps))] * 2
-        + [pltpu.SemaphoreType.DMA((pieces_a, batch_count - 1))] * 2
-        + [pltpu.SemaphoreType.DMA((batch_count - 1,))] * 2
+        + [sems((2, max(pieces_a, pieces_b), steps))] * 2
+        + [sems((pieces_a, batch_count - 1))] * 2
+        + [sems((pieces_b, batch_count - 1))] * 2
     )
+    spread, slots = piece_orders(tok, scene_count)
+    moves = [jnp.asarray(x, BF16) for x in (spread, spread.T, slots, slots.T)]
+    grad_scale = float(tok * scene_count * batch_count) ** -0.5
+    vmem, anywhere = pl.BlockSpec(memory_space=pltpu.VMEM), pl.BlockSpec(memory_space=pl.ANY)
     return pl.pallas_call(
-        functools.partial(mlp_reduce_kernel, grad_scale, orders_ab, batch_count),
+        functools.partial(block_kernel, grad_scale, orders_ab, batch_count, width // heads),
+        in_specs=[vmem] * 3 + [anywhere] * 5 + [vmem] * 5,
         out_shape=(
             shape_of(tok, width),
             shape_of(tok, width),
@@ -408,8 +620,7 @@
         compiler_params=pltpu.CompilerParams(
             vmem_limit_bytes=VMEM_LIMIT, collective_id=0, has_side_effects=True
         ),
-        cost_estimate=pl.CostEstimate(flops=10**10, bytes_accessed=4000000, transcendentals=0),
-    )(first, returned, cot, w_up, w_down)
+    )(local, offsets, conv_weight, w_up, w_down, w_qkv, w_out, cot, score_bias, *moves)
 
 
 def shape_of(*dims):
@@ -443,6 +654,14 @@
     heads = score_bias.shape[0]
     scene_count = lax.axis_size("scene")
     batch_count = lax.axis_size("batch")
+    if can_fuse(
+        tok, width, width // heads, conv_weight.shape[0], hidden_width, scene_count, batch_count
+    ):
+        block_out, grad_mid, *grads = fused(
+            scene_count, batch_count, local, nbr_offset[:, 0, :], cotangent[0],
+            conv_weight, w_qkv, w_out, score_bias, w_up, w_down,
+        )
+        return (block_out[None], grad_mid[None], *grads)
     forward = [(i, i + 1) for i in range(scene_count - 1)]
     backward = [(target, source) for source, target in forward]
     low = lax.ppermute(local[tok - HALO :], "scene", forward)
@@ -475,11 +694,6 @@
         mixed.reshape(per, scene_count, count, width), "scene", split_axis=1, concat_axis=1, tiled=True
     ).reshape(tok, width)
     grad_scale = float(tok * scene_count * batch_count) ** -0.5
-    if can_fuse(width, hidden_width, scene_count, batch_count):
-        block_out, grad_mid, *grads = mlp_reduced(
-            grad_scale, scene_count, batch_count, first, returned, cotangent[0], w_up, w_down
-        )
-        return (block_out[None], grad_mid[None], *grads)
     block_out, grad_mid, grad_up, grad_down = call(
         functools.partial(mlp_kernel, grad_scale),
         (

time: 120 us -> 85.9 us (0.72)
  blocking collectives: 12.8 us -> 0 us
  starting transfers between devices: 12.4 us -> 0 us
  Pallas kernels: 69 us -> 78.4 us
  local copies, waits for them, and re-layouts: 15.7 us -> 6.56 us
  waiting for transfers between devices: 8.75 us -> 0 us
    all_to_all x1 -> x0, blocking collectives: 12.8 us -> none  [on_device(): lax.all_to_all(mixed.reshape(per, scene_count, count, width), 'scene', sp...]
    pallas_call x3 -> x1, Pallas kernels: 69 us -> 78.4 us  [fused(): pl.pallas_call(functools.partial(block_kernel, grad_scale, orders_ab, bat...]
    all_to_all x1 -> x0, waiting for transfers between devices: 8.74 us -> none  [on_device(): lax.all_to_all(blocks, 'scene', split_axis=1, concat_axis=1, tiled=True)]
    all_to_all x1 -> x0, starting transfers between devices: 8.08 us -> none  [on_device(): lax.all_to_all(blocks, 'scene', split_axis=1, concat_axis=1, tiled=True)]
    reshape x6 -> x0, local copies, waits for them, and re-layouts: 5.64 us -> none  [the longest x2 2.37 us: on_device(): blocks = normed.reshape(per, scene_count, count, width)]
    ppermute x2 -> x0, starting transfers between devices: 4.33 us -> none  [the longest x1 3.04 us: on_device(): low = lax.ppermute(local[tok - HALO:], 'scene', forward)]
    another operation x2 -> x0, local copies, waits for them, and re-layouts: 1.69 us -> none  [on_device(): bias = jnp.tile(score_bias, (1, 1, TILE // GROUP))]
    unnamed x15 -> x9, local copies, waits for them, and re-layouts: 7.22 us -> 6.56 us
  transfers between devices with their start and end apart: 3 -> 0, of which waited for: 1 -> 0; matrix products, arithmetic and copies ran while one was open for 3% -> 0% of each run, Pallas kernels for 0% -> 0%
where the time goes in v2:
time: 85.9 us; the launch traced here: 85.6 us
  Pallas kernels  78.4 us (91%)
  local copies, waits for them, and re-layouts  6.56 us (8%)
    pallas_call x1, Pallas kernels, fused(): pl.pallas_call(functools.partial(block_kernel, grad_scale, orders_ab, bat...  78.4 us
    unnamed x9, local copies, waits for them, and re-layouts  6.56 us

profile of v2, /device:TPU:0, one launch (start us, length us, event | category | flops | bytes accessed | tf_op | source)
XLA Modules:
  0.0 85.6 jit_solution(14192744786492037304)
XLA Ops:
  0.6 1.4 %copy.19 = s32[27,1,384]{2,0,1:T(8,128)} copy(s32[27,1,384]{2,1,0:T(1,128)} %param.14) | data formatting | bytes 82944
  2.0 78.4 %shard_map.156 = (f32[384,384]{1,0:T(8,128)}, f32[384,384]{1,0:T(8,128)}, f32[48,384]{1,0:T(8,128)}, f32[192,96]{1,0:T(8,128)}) custom-call(f32[384,384]{1,0:T(8,128)} %bitcast.7, s32[27,384]{1,0:T(8,128)} %bitcast.11, f32[27,384]{1,0:T(8,128)} %weight_ref.1, f32[384,1536]{1,0:T(8,128)} %up_hbm.1, f32[1536,384]{1,0:T(8,128)} %down_hbm.1, ...), custom_call_target="tpu_custom_call" | custom-call | tf_op jit(solution)/shard_map/pallas_call | solution.py:610
  80.5 0.0 copy-start.1
  80.5 0.0 copy-start
  80.5 2.0 %copy.24 = f32[1,384,384]{2,1,0:T(8,128)} copy(f32[1,384,384]{2,1,0:T(8,128)} %bitcast.10) | data formatting | bytes 1179648
  82.4 1.9 %copy.25 = f32[1,384,384]{2,1,0:T(8,128)} copy(f32[1,384,384]{2,1,0:T(8,128)} %bitcast.9) | data formatting | bytes 1179648
  84.4 0.0 copy-done.1
  84.4 0.6 copy.26
  85.0 0.0 copy-done
  85.0 0.6 copy.27
Async XLA Ops:
  80.5 3.9 %copy-start.1 = (f32[48,384]{1,0:T(8,128)S(1)}, f32[48,384]{1,0:T(8,128)}, u32[]{:S(2)}) copy-start(f32[48,384]{1,0:T(8,128)} %get-tuple-element.18) | copy-start | bytes 221188
  80.5 4.5 %copy-start = (f32[192,96]{1,0:T(8,128)S(1)}, f32[192,96]{1,0:T(8,128)}, u32[]{:S(2)}) copy-start(f32[192,96]{1,0:T(8,128)} %get-tuple-element.19) | copy-start | bytes 221188

commit v3 on v2

--- a/solution.py
+++ b/solution.py
@@ -193,7 +193,7 @@
     wqkv3, wout3, bias_tile, up_hi, up_lo, down_hi, down_lo,
     n_left, c_left, nt_left, ct_left, slope, act_hi, act_lo, gh_hi, gh_lo,
     acc_a, acc_b, recv_a, recv_b, zrecv_a, zsend_b, zrecv_b,
-    send_sem, recv_sem, za_send, za_recv, zb_send, zb_recv,
+    send_sem, recv_sem, core_send, core_recv, za_send, za_recv, zb_send, zb_recv,
 ):
     tok, width = local_ref.shape
     hidden_width = up_ref.shape[1]
@@ -249,10 +249,6 @@
         to_scene(local_ref.at[pl.ds(tok - HALO, HALO)], low, halo_send.at[0], halo_recv.at[0], scenes[0]),
         to_scene(local_ref.at[pl.ds(0, HALO)], high, halo_send.at[1], halo_recv.at[1], scenes[-1]),
     ]
-    pl.semaphore_wait(barrier, scene_count + batch_count - 2)
-    for copy in halo:
-        start(copy)
-
     taps = weight_ref.shape[0]
     span = TILE + 2 * HALO
 
@@ -263,10 +259,15 @@
 
     extend(HALO, local_ref[...])
     for t in range(tiles):
-        piece = offset_ref[:, t * TILE : (t + 1) * TILE]
+        piece = offset_ref[:, 0, t * TILE : (t + 1) * TILE]
         piece = jnp.where(piece > HALO, 4 * TILE, piece).astype(F32)
         piece = jnp.concatenate([piece, jnp.zeros((TILE - taps, TILE), F32)], axis=0)
         off_t[t * TILE : (t + 1) * TILE, :] = piece.T
+    for h in range(bias_ref.shape[0]):
+        bias_tile[h] = jnp.concatenate([bias_ref[h]] * (TILE // GROUP), axis=1)
+    pl.semaphore_wait(barrier, scene_count + batch_count - 2)
+    for copy in halo:
+        start(copy)
     base = (
         lax.broadcasted_iota(jnp.int32, (TILE, span), 1)
         - lax.broadcasted_iota(jnp.int32, (TILE, span), 0)
@@ -315,8 +316,6 @@
         wqkv3[:, at] = right3(wqkv_ref[:, at])
     loads[1].wait()
     wout3[...] = right3(wout_ref[...])
-    for h in range(bias_ref.shape[0]):
-        bias_tile[h] = jnp.concatenate([bias_ref[h]] * (TILE // GROUP), axis=1)
     shape = (TILE, TILE)
     same = (lax.broadcasted_iota(jnp.int32, shape, 0) ^ lax.broadcasted_iota(jnp.int32, shape, 1)) < GROUP
     away = jnp.where(same, 0.0, -1e30)
@@ -410,7 +409,12 @@
             device_id_type=MESH,
         )
 
+    done = set()
+
     def advance(stream, q, i):
+        if (stream, q, i) in done:
+            return
+        done.add((stream, q, i))
         halving(stream, q, i).wait_recv()
         mine = (q, *kept(stream, i + 1))
         accs[stream][mine] = accs[stream][mine] + recvs[stream][i][q]
@@ -433,8 +437,34 @@
     n_left[...] = left3(normed)
 
     chunk = 2 * rows_b
-    for c in range(hidden_width // chunk):
-        at = slice(c * chunk, (c + 1) * chunk)
+    chunks = hidden_width // chunk
+    top = values[steps - 1]
+
+    def chunk_at(j):
+        return lax.rem((1 - top) * (chunks // 2) + j, chunks)
+
+    def chunk_bits(j):
+        return tuple((chunk_at(j) // 2 ** (bit - 1)) % 2 for bit in orders_ab[1][1:])
+
+    def early(q, j):
+        return to_scene(
+            acc_b.at[(q, 1 - values[0], *chunk_bits(j))],
+            recv_b[0].at[(q, *chunk_bits(j))],
+            core_send.at[q, j],
+            core_recv.at[q, j],
+            partners[0],
+        )
+
+    def add_early(q, half):
+        for j in range(half * (chunks // 2), (half + 1) * (chunks // 2)):
+            early(q, j).wait_recv()
+        which = (1 - top, top)[half]
+        acc_b[q, values[0], which] = acc_b[q, values[0], which] + recv_b[0][q, which]
+        if half == 0:
+            start(halving(1, q, 1))
+
+    for j in range(chunks):
+        at = pl.ds(pl.multiple_of(chunk_at(j) * chunk, chunk), chunk)
         hidden = dot(n_left[...], jnp.concatenate([up_hi[:, at], up_lo[:, at], up_hi[:, at]], axis=0))
         cdf = 0.5 * (1.0 + lax.erf(hidden * (0.5**0.5)))
         density = jnp.exp(-0.5 * hidden * hidden) * ((2.0 * np.pi) ** -0.5)
@@ -444,11 +474,14 @@
         act_lo[:, at] = lo
         grad = dot(ct_left[...], jnp.concatenate([hi, lo, hi], axis=0)).T
         for half in range(2):
-            block = bits_of(2 * c + half, orders_ab[1])
             for q in range(pieces_b):
-                acc_b[(q, *block)] = grad[half * rows_b : (half + 1) * rows_b, q * TILE : (q + 1) * TILE]
-    for q in range(pieces_b):
-        start(halving(1, q, 0))
+                acc_b[(q, half, *chunk_bits(j))] = grad[
+                    half * rows_b : (half + 1) * rows_b, q * TILE : (q + 1) * TILE
+                ]
+        for q in range(pieces_b):
+            start(early(q, j))
+        if j >= chunks // 2 and j - chunks // 2 < pieces_b:
+            add_early(j - chunks // 2, 0)
     nt_left[...] = left3(normed.T * grad_scale)
 
     part = batch_count * TILE
@@ -471,10 +504,14 @@
                 ]
         start(halving(0, q, 0))
         if q == 0:
+            for p in range(min(chunks // 2 + chunks % 2, pieces_b), pieces_b):
+                add_early(p, 0)
             for p in range(pieces_b):
-                advance(1, p, 0)
+                add_early(p, 1)
         else:
             advance(0, q - 1, 0)
+        if q == 1:
+            advance(1, 0, 1)
 
     out_ref[...] = (
         middle
@@ -483,7 +520,8 @@
         + dot(act_lo[...], down_hi[...])
     )
     advance(0, pieces_a - 1, 0)
-    advance(1, 0, 1)
+    for p in range(pieces_b - 1):
+        advance(1, p, 1)
     advance(0, 0, 1)
 
     g = jnp.zeros((tok, width), F32)
@@ -495,10 +533,13 @@
     along = jnp.mean(g * normed, axis=-1, keepdims=True)
     mid_ref[...] = cot_ref[...] + scale * (g - jnp.mean(g, axis=-1, keepdims=True) - normed * along)
 
+    advance(1, pieces_b - 1, 1)
+    if pieces_a > 2:
+        advance(0, 1, 1)
     for i in range(1, steps):
         for q in range(max(pieces_a, pieces_b)):
             for stream, count in ((1, pieces_b), (0, pieces_a)):
-                if q < count and not (i == 1 and q == 0):
+                if q < count:
                     advance(stream, q, i)
     rows = []
     for q in range(pieces_b):
@@ -550,6 +591,36 @@
     slots = np.zeros((TILE, TILE), np.float32)
     slots[row, row % GROUP * some + row // GROUP] = 1.0
     return spread, slots
+
+
+def pieces_of(ref, count):
+    rows = ref.shape[0] // count
+    return [ref.at[pl.ds(i * rows, rows)] for i in range(count)]
+
+
+def hand_over_kernel(*refs):
+    sources, targets, sem = refs[:4], refs[4:8], refs[8]
+    copies = []
+    for source, target in zip(sources, targets):
+        count = 4 if source.shape[0] % 32 == 0 and source.shape[0] >= 256 else 1
+        for a, b in zip(pieces_of(source, count), pieces_of(target, count)):
+            copies.append(pltpu.make_async_copy(a, b, sem.at[len(copies)]))
+    for copy in copies:
+        copy.start()
+    for copy in copies:
+        copy.wait()
+
+
+def hand_over(results):
+    anywhere = pl.BlockSpec(memory_space=pl.ANY)
+    return pl.pallas_call(
+        hand_over_kernel,
+        in_specs=[anywhere] * 4,
+        out_specs=[anywhere] * 4,
+        out_shape=tuple(shape_of(*x.shape) for x in results),
+        scratch_shapes=[pltpu.SemaphoreType.DMA((16,))],
+        compiler_params=pltpu.CompilerParams(vmem_limit_bytes=VMEM_LIMIT),
+    )(*results)
 
 
 def fused(scene_count, batch_count, local, offsets, cot, conv_weight, w_qkv, w_out, score_bias, w_up, w_down):
@@ -600,6 +671,7 @@
             pltpu.VMEM((pieces_b, batch_count - 1, sub, padded), F32),
         ]
         + [sems((2, max(pieces_a, pieces_b), steps))] * 2
+        + [sems((pieces_b, scene_count // 2))] * 2
         + [sems((pieces_a, batch_count - 1))] * 2
         + [sems((pieces_b, batch_count - 1))] * 2
     )
@@ -607,7 +679,7 @@
     moves = [jnp.asarray(x, BF16) for x in (spread, spread.T, slots, slots.T)]
     grad_scale = float(tok * scene_count * batch_count) ** -0.5
     vmem, anywhere = pl.BlockSpec(memory_space=pltpu.VMEM), pl.BlockSpec(memory_space=pl.ANY)
-    return pl.pallas_call(
+    results = pl.pallas_call(
         functools.partial(block_kernel, grad_scale, orders_ab, batch_count, width // heads),
         in_specs=[vmem] * 3 + [anywhere] * 5 + [vmem] * 5,
         out_shape=(
@@ -621,6 +693,7 @@
             vmem_limit_bytes=VMEM_LIMIT, collective_id=0, has_side_effects=True
         ),
     )(local, offsets, conv_weight, w_up, w_down, w_qkv, w_out, cot, score_bias, *moves)
+    return hand_over(results)
 
 
 def shape_of(*dims):
@@ -658,7 +731,7 @@
         tok, width, width // heads, conv_weight.shape[0], hidden_width, scene_count, batch_count
     ):
         block_out, grad_mid, *grads = fused(
-            scene_count, batch_count, local, nbr_offset[:, 0, :], cotangent[0],
+            scene_count, batch_count, local, nbr_offset, cotangent[0],
             conv_weight, w_qkv, w_out, score_bias, w_up, w_down,
         )
         return (block_out[None], grad_mid[None], *grads)

time: 85.9 us -> 122 us (1.42)
  Pallas kernels: 78.4 us -> 121 us
  local copies, waits for them, and re-layouts: 6.56 us -> 0 us
    pallas_call x0 -> x1, Pallas kernels: none -> 42.2 us  [hand_over(): pl.pallas_call(hand_over_kernel, in_specs=[anywhere] * 4, out_specs=[anyw...]
    unnamed x9 -> x0, local copies, waits for them, and re-layouts: 6.56 us -> none
where the time goes in v3:
time: 122 us
  Pallas kernels  121 us (99%)
    pallas_call x1, Pallas kernels, fused(): pl.pallas_call(functools.partial(block_kernel, grad_scale, orders_ab, bat...  79 us
    pallas_call x1, Pallas kernels, hand_over(): pl.pallas_call(hand_over_kernel, in_specs=[anywhere] * 4, out_specs=[anyw...  42.2 us

profile of v3, /device:TPU:0, one launch (start us, length us, event | category | flops | bytes accessed | tf_op | source)
XLA Modules:
  0.0 122.0 jit_solution(12017741104150496285)
XLA Ops:
  0.6 79.0 %shard_map.156 = (f32[384,384]{1,0:T(8,128)}, f32[384,384]{1,0:T(8,128)}, f32[48,384]{1,0:T(8,128)}, f32[192,96]{1,0:T(8,128)}) custom-call(f32[384,384]{1,0:T(8,128)} %bitcast.4, s32[27,1,384]{2,1,0:T(1,128)} %offset_ref.1, f32[27,384]{1,0:T(8,128)} %weight_ref.1, f32[384,1536]{1,0:T(8,128)} %up_hbm.1, f32[1536,384]{1,0:T(8,128)} %down_hbm.1, ...), custom_call_target="tpu_custom_call" | custom-call | tf_op jit(solution)/shard_map/pallas_call | solution.py:682
  79.6 42.2 %shard_map.157 = (f32[384,384]{1,0:T(8,128)}, f32[384,384]{1,0:T(8,128)}, f32[48,384]{1,0:T(8,128)}, f32[192,96]{1,0:T(8,128)}) custom-call(f32[384,384]{1,0:T(8,128)} %get-tuple-element.12.refs_0_, f32[384,384]{1,0:T(8,128)} %get-tuple-element.13.refs_1_, f32[48,384]{1,0:T(8,128)} %get-tuple-element.14.refs_2_, f32[192,96]{1,0:T(8,128)} %get-tuple-element.15.refs_3_), custom_call_target="tpu_custom_call" | custom-call | tf_op jit(solution)/shard_map/pallas_call | solution.py:616

commit v4 on v3

--- a/solution.py
+++ b/solution.py
@@ -593,32 +593,15 @@
     return spread, slots
 
 
-def pieces_of(ref, count):
-    rows = ref.shape[0] // count
-    return [ref.at[pl.ds(i * rows, rows)] for i in range(count)]
-
-
 def hand_over_kernel(*refs):
-    sources, targets, sem = refs[:4], refs[4:8], refs[8]
-    copies = []
-    for source, target in zip(sources, targets):
-        count = 4 if source.shape[0] % 32 == 0 and source.shape[0] >= 256 else 1
-        for a, b in zip(pieces_of(source, count), pieces_of(target, count)):
-            copies.append(pltpu.make_async_copy(a, b, sem.at[len(copies)]))
-    for copy in copies:
-        copy.start()
-    for copy in copies:
-        copy.wait()
+    for source, target in zip(refs[:4], refs[4:]):
+        target[...] = source[...]
 
 
 def hand_over(results):
-    anywhere = pl.BlockSpec(memory_space=pl.ANY)
     return pl.pallas_call(
         hand_over_kernel,
-        in_specs=[anywhere] * 4,
-        out_specs=[anywhere] * 4,
         out_shape=tuple(shape_of(*x.shape) for x in results),
-        scratch_shapes=[pltpu.SemaphoreType.DMA((16,))],
         compiler_params=pltpu.CompilerParams(vmem_limit_bytes=VMEM_LIMIT),
     )(*results)
 

time: 122 us -> 82.2 us (0.67)
  Pallas kernels: 121 us -> 81.4 us
    pallas_call x1, Pallas kernels: 42.2 us -> 2.37 us  [hand_over(): pl.pallas_call(hand_over_kernel, out_shape=tuple((shape_of(*x.shape) for...]
where the time goes in v4:
time: 82.2 us; the launch traced here: 82 us
  Pallas kernels  81.4 us (99%)
    pallas_call x1, Pallas kernels, fused(): pl.pallas_call(functools.partial(block_kernel, grad_scale, orders_ab, bat...  79 us
    pallas_call x1, Pallas kernels, hand_over(): pl.pallas_call(hand_over_kernel, out_shape=tuple((shape_of(*x.shape) for...  2.37 us

profile of v4, /device:TPU:0, one launch (start us, length us, event | category | flops | bytes accessed | tf_op | source)
XLA Modules:
  0.0 82.0 jit_solution(2728097416362897512)
XLA Ops:
  0.6 79.0 %shard_map.156 = (f32[384,384]{1,0:T(8,128)}, f32[384,384]{1,0:T(8,128)}, f32[48,384]{1,0:T(8,128)}, f32[192,96]{1,0:T(8,128)}) custom-call(f32[384,384]{1,0:T(8,128)} %bitcast.4, s32[27,1,384]{2,1,0:T(1,128)} %offset_ref.1, f32[27,384]{1,0:T(8,128)} %weight_ref.1, f32[384,1536]{1,0:T(8,128)} %up_hbm.1, f32[1536,384]{1,0:T(8,128)} %down_hbm.1, ...), custom_call_target="tpu_custom_call" | custom-call | tf_op jit(solution)/shard_map/pallas_call | solution.py:665
  79.6 2.4 %shard_map.157 = (f32[384,384]{1,0:T(8,128)}, f32[384,384]{1,0:T(8,128)}, f32[48,384]{1,0:T(8,128)}, f32[192,96]{1,0:T(8,128)}) custom-call(f32[384,384]{1,0:T(8,128)} %get-tuple-element.12.refs_0_, f32[384,384]{1,0:T(8,128)} %get-tuple-element.13.refs_1_, f32[48,384]{1,0:T(8,128)} %get-tuple-element.14.refs_2_, f32[192,96]{1,0:T(8,128)} %get-tuple-element.15.refs_3_), custom_call_target="tpu_custom_call" | custom-call | tf_op jit(solution)/shard_map/pallas_call | solution.py:602
